TPU v7x, 32 devices: a whole 2x2x4 slice. The times are simulated.
32 devices in a mesh: grp: 4 (over y, x), cell: 8 (over z, core).
Axes of the slice: x: 2, y: 2, z: 4, core: 2. Of those that a mesh axis runs over, the one named last changes fastest.
Arguments:
- expression: bfloat16 [2000, 16384], P(None, ('grp', 'cell')), may hold values from 0.019897461 to 4
- dataset_id: int32 [16384], P(('grp', 'cell')), may hold values from 0 to 3, as said below
- dataset_map: int32 [4], P('grp'), may hold values from 0 to 3, as said below
- sweep_count: int32 [4], replicated, may hold values from 2 to 4
- picks: int32 [2, 4096], P(None, ('grp', 'cell')), may hold values from 0 to 511
- shared_init: float32 [64, 2000], replicated, may hold values from 0.004 to 0.06
- specific_init: float32 [4, 64, 2000], P('grp'), may hold values from 0.001 to 0.02
Outputs:
- loadings: float32 [2, 64, 4096], P(None, None, ('grp', 'cell'))
- shared_basis: float32 [64, 2000], replicated
- specific_basis: float32 [4, 64, 2000], P('grp')
Inputs may be any that keep to these rules, and one draw needn't show every extreme that they name: `dataset_map`: a permutation of the datasets; entry g is the one dataset of device group g. `dataset_id`: every cell held by the devices of group g belongs to one of the datasets that dataset_map gives to group g. `picks`: an index into the cells held by the device that holds the slot; a cell may be picked more than once.
All inputs are finite; a program needn't handle non-finite values.
Results may differ from a plain program's by a relative error of at most 0.0065.
The roundings to bfloat16 on the way count: a program that leaves them out, or rounds other values in their place, can miss the bound.
Values sent between devices are 32-bit elements; how exact they have to be, the bound alone decides.
A program may use at most 128 MiB of HBM per device.

v0:
```python
import functools

import jax
import jax.numpy as jnp
from jax import lax
from jax.experimental import pallas as pl
from jax.experimental.pallas import tpu as pltpu
from jax.sharding import PartitionSpec as P

K = 64
SWEEPS = 4
LANES = 128
BLOCK = 8

EPSILON = 1e-06
LAMBDA = 5.0
HIGHEST = lax.Precision.HIGHEST
MESH = pl.DeviceIdType.MESH
TRANSPOSED = (((1,), (1,)), ((), ()))


def identity_of(rows, columns):
    return (
        lax.broadcasted_iota(jnp.int32, (rows, columns), 0)
        == lax.broadcasted_iota(jnp.int32, (rows, columns), 1)
    ).astype(jnp.float32)


def cell_kernel(
    scalars, expression, picks, shared, specific,
    loadings_out, stats_out, grams_out, shared_out, specific_out,
    table, padded,
):
    rounds, chunks, _, width = stats_out.shape
    genes = shared.shape[1]
    pool = expression.shape[1]
    cells = picks.shape[1]
    per_round = cells // rounds

    padded[...] = jnp.zeros_like(padded)
    own = pl.ds(pl.multiple_of(scalars[1] * width, LANES), width)
    for source, place in ((shared, shared_out), (specific, specific_out)):
        padded[:, :genes] = source[...]
        place[...] = padded[:, own]

    combined = shared[...] + specific[...]
    gram = lax.dot_general(
        combined, combined, TRANSPOSED, precision=HIGHEST, preferred_element_type=jnp.float32
    ) + LAMBDA * lax.dot_general(
        specific[...], specific[...], TRANSPOSED, precision=HIGHEST,
        preferred_element_type=jnp.float32,
    )
    chosen = (
        lax.broadcasted_iota(jnp.int32, (pool, cells), 0) == picks[...]
    ).astype(jnp.bfloat16)
    data = jnp.dot(expression[...], chosen, preferred_element_type=jnp.float32).astype(jnp.bfloat16)
    target = jnp.dot(combined.astype(jnp.bfloat16), data, preferred_element_type=jnp.float32)

    eye = identity_of(K, K)
    divisor = jnp.sum(gram * eye, axis=1, keepdims=True) + EPSILON
    pull = eye - gram / divisor
    for factor in range(K):
        table[factor] = jnp.broadcast_to(pull[:, factor : factor + 1], (K, LANES))
    start = target / divisor
    blocks = K // BLOCK
    tiles = cells // LANES
    row = lax.broadcasted_iota(jnp.int32, (BLOCK, LANES), 0)

    def sweep(_, state):
        wish, held = [list(part) for part in state]
        for factor in range(K):
            block, place = divmod(factor, BLOCK)
            for tile in range(tiles):
                at = block * tiles + tile
                renewed = jnp.maximum(wish[at], 0.0)
                change = renewed - held[at]
                change = jnp.broadcast_to(change[place : place + 1], (BLOCK, LANES))
                held[at] = jnp.where(row == place, renewed, held[at])
                for other in range(blocks):
                    to = other * tiles + tile
                    wish[to] = (
                        wish[to]
                        + table[factor, other * BLOCK : (other + 1) * BLOCK, :] * change
                    )
        return tuple(wish), tuple(held)

    first = tuple(
        start[block * BLOCK : (block + 1) * BLOCK, tile * LANES : (tile + 1) * LANES]
        for block in range(blocks)
        for tile in range(tiles)
    )
    zero = tuple(jnp.zeros((BLOCK, LANES), jnp.float32) for _ in first)
    _, held = lax.fori_loop(0, jnp.minimum(scalars[0], SWEEPS), sweep, (first, zero))

    per_tile = per_round // LANES
    for round_index in range(rounds):
        parts = [
            jnp.concatenate([held[block * tiles + tile] for block in range(blocks)], axis=0)
            for tile in range(round_index * per_tile, (round_index + 1) * per_tile)
        ]
        loads = parts[0] if per_tile == 1 else jnp.concatenate(parts, axis=1)
        loadings_out[round_index] = loads
        grams_out[round_index] = jnp.zeros((K, LANES), jnp.float32)
        grams_out[round_index, :, :K] = lax.dot_general(
            loads, loads, TRANSPOSED, precision=HIGHEST, preferred_element_type=jnp.float32
        )
        stats = lax.dot_general(
            loads.astype(jnp.bfloat16),
            data[:, round_index * per_round : (round_index + 1) * per_round],
            TRANSPOSED,
            preferred_element_type=jnp.float32,
        )
        for chunk in range(chunks):
            low = chunk * width
            high = min(low + width, genes)
            if high < low + width:
                stats_out[round_index, chunk] = jnp.zeros((K, width), jnp.float32)
            if high > low:
                stats_out[round_index, chunk, :, : high - low] = stats[:, low:high]


def renew(current, residual, gram, scale, wish_ref, pull_ref, out_ref):
    width = current.shape[1]
    eye = identity_of(K, LANES)
    scaled = scale * gram
    divisor = jnp.maximum(jnp.sum(scaled * eye, axis=1, keepdims=True), 1.0)
    pull = eye - scaled / divisor
    wish_ref[...] = current + residual / divisor
    out_ref[...] = current
    row = lax.broadcasted_iota(jnp.int32, (BLOCK, width), 0)

    def step(block, carry):
        turned = pltpu.roll(pull, LANES - BLOCK * block, axis=1)
        pull_ref[...] = turned
        rows = pl.ds(pl.multiple_of(block * BLOCK, BLOCK), BLOCK)
        near = pull_ref[rows, :]
        wish = wish_ref[rows, :]
        held = out_ref[rows, :]
        total = wish_ref[...]
        for place in range(BLOCK):
            renewed = jnp.maximum(wish, 0.0)
            change = jnp.broadcast_to((renewed - held)[place : place + 1], (BLOCK, width))
            held = jnp.where(row == place, renewed, held)
            wish = wish + jnp.broadcast_to(near[:, place : place + 1], (BLOCK, width)) * change
            wide = jnp.concatenate([change] * (K // BLOCK), axis=0)
            total = total + jnp.broadcast_to(turned[:, place : place + 1], (K, width)) * wide
        wish_ref[...] = total
        out_ref[rows, :] = held
        return carry

    lax.fori_loop(0, K // BLOCK, step, 0)


def basis_kernel(
    groups, cell_count, stats, grams, shared, specific, shared_out, specific_out,
    sib_stats, sib_grams, along, arrived, sent, gathered, wide_shared, wide_specific,
    wish_ref, pull_ref, shared_ref, specific_ref,
    sib_send, sib_recv, along_send, along_recv, grp_send, grp_recv,
    out_send, out_recv, pair_send, pair_recv,
):
    rounds, chunks, _, width = stats.shape
    layers = cell_count // 2
    grp = lax.axis_index("grp")
    cell = lax.axis_index("cell")
    layer = cell // 2
    core = cell % 2
    sibling = layer * 2 + (1 - core)
    mine = core * layers + layer

    def layer_at(offset):
        return (layer + offset) % layers

    barrier = pltpu.get_barrier_semaphore()
    pl.semaphore_signal(barrier, inc=1, device_id={"cell": sibling}, device_id_type=MESH)
    for offset in range(1, layers):
        pl.semaphore_signal(
            barrier, inc=1, device_id={"cell": layer_at(offset) * 2 + core}, device_id_type=MESH
        )
    for offset in range(1, groups):
        pl.semaphore_signal(
            barrier, inc=1, device_id={"grp": (grp + offset) % groups}, device_id_type=MESH
        )
    pl.semaphore_wait(barrier, 1 + (layers - 1) + (groups - 1))

    started = []

    def send(source, place, send_sem, recv_sem, device):
        copy = pltpu.make_async_remote_copy(
            src_ref=source, dst_ref=place, send_sem=send_sem, recv_sem=recv_sem,
            device_id=device, device_id_type=MESH,
        )
        copy.start()
        started.append(copy)
        return copy

    pair = []
    for r in range(rounds):
        pair.append((
            send(grams.at[r], sib_grams.at[r], sib_send.at[r, 0], sib_recv.at[r, 0],
                 {"cell": sibling}),
            send(stats.at[r, pl.ds((1 - core) * layers, layers)], sib_stats.at[r],
                 sib_send.at[r, 1], sib_recv.at[r, 1], {"cell": sibling}),
        ))

    across = []
    for r in range(rounds):
        for copy in pair[r]:
            copy.wait_recv()
        gram_sum = grams[r] + sib_grams[r]
        copies = []
        for offset in range(layers - 1, -1, -1):
            at = layer_at(offset)
            along[r, offset, :, :width] = stats[r, core * layers + at] + sib_stats[r, at]
            along[r, offset, :, width:] = gram_sum
            if offset:
                copies.append(send(
                    along.at[r, offset], arrived.at[r, offset - 1],
                    along_send.at[r, offset - 1], along_recv.at[r, offset - 1],
                    {"cell": at * 2 + core},
                ))
        across.append(copies)

    shared_ref[...] = shared[...]
    specific_ref[...] = specific[...]
    stat_sum = None
    for r in range(rounds):
        for copy in across[r]:
            copy.wait_recv()
        increase = along[r, 0]
        for offset in range(1, layers):
            increase = increase + arrived[r, offset - 1]
        stat_sum = increase if stat_sum is None else stat_sum + increase
        stat, gram = stat_sum[:, :width], stat_sum[:, width:]
        small = gram[:, :K]
        before = specific_ref[...]
        pulled = jnp.dot(small, before, precision=HIGHEST, preferred_element_type=jnp.float32)
        sent[r, :, :width] = stat - pulled
        sent[r, :, width:] = gram
        copies = [
            send(sent.at[r], gathered.at[r, offset - 1], grp_send.at[r, offset - 1],
                 grp_recv.at[r, offset - 1], {"grp": (grp + offset) % groups})
            for offset in range(1, groups)
        ]
        for copy in copies:
            copy.wait_recv()
        total = sent[r]
        for offset in range(1, groups):
            total = total + gathered[r, offset - 1]
        carried, gram_total = total[:, :width], total[:, width:]
        old = shared_ref[...]
        residual = carried - jnp.dot(
            gram_total[:, :K], old, precision=HIGHEST, preferred_element_type=jnp.float32
        )
        renew(old, residual, gram_total, 1.0, wish_ref, pull_ref, shared_ref)
        last = r == rounds - 1
        if last:
            wide_shared[mine] = shared_ref[...]
            shared_copies = spread(
                send, wide_shared, 0, mine, core, layers, layer_at, sibling,
                out_send, out_recv, pair_send, pair_recv,
            )
        residual = stat - (1.0 + LAMBDA) * pulled - jnp.dot(
            small, shared_ref[...], precision=HIGHEST, preferred_element_type=jnp.float32
        )
        renew(before, residual, gram, 1.0 + LAMBDA, wish_ref, pull_ref, specific_ref)
        if last:
            wide_specific[mine] = specific_ref[...]
            specific_copies = spread(
                send, wide_specific, 1, mine, core, layers, layer_at, sibling,
                out_send, out_recv, pair_send, pair_recv,
            )

    waiting = []
    for index, (wide, copies) in enumerate(
        ((wide_shared, shared_copies), (wide_specific, specific_copies))
    ):
        fetched = [copies[0]]
        for offset in range(1, layers):
            copies[offset].wait_recv()
            came = core * layers + layer_at(layers - offset)
            fetched.append(send(
                wide.at[came], wide.at[came], pair_send.at[index, offset],
                pair_recv.at[index, offset], {"cell": sibling},
            ))
        waiting.append(fetched)
    genes = shared_out.shape[1]
    for wide, fetched, out in (
        (wide_shared, waiting[0], shared_out), (wide_specific, waiting[1], specific_out)
    ):
        for copy in fetched:
            copy.wait_recv()
        for chunk in range(chunks):
            low = chunk * width
            high = min(low + width, genes)
            if high > low:
                out[:, low:high] = wide[chunk, :, : high - low]
    for copy in started:
        copy.wait_send()


def spread(
    send, wide, index, mine, core, layers, layer_at, sibling,
    out_send, out_recv, pair_send, pair_recv,
):
    copies = {}
    for offset in range(layers - 1, 0, -1):
        copies[offset] = send(
            wide.at[mine], wide.at[mine], out_send.at[index, offset - 1],
            out_recv.at[index, offset - 1], {"cell": layer_at(offset) * 2 + core},
        )
    copies[0] = send(
        wide.at[mine], wide.at[mine], pair_send.at[index, 0], pair_recv.at[index, 0],
        {"cell": sibling},
    )
    return copies


def on_device(
    groups, cell_count, expression, dataset_id, dataset_map, sweep_count, picks,
    shared_init, specific_init,
):
    genes = expression.shape[0]
    rounds, per_round = picks.shape
    layers = cell_count // 2
    width = -(-genes // (cell_count * LANES)) * LANES
    cell = lax.axis_index("cell")
    limit = jnp.sum(
        jnp.where(jnp.arange(sweep_count.shape[0]) == dataset_map[0], sweep_count, 0)
    )
    mine = (cell % 2) * layers + cell // 2
    scalars = jnp.stack([limit, mine]).astype(jnp.int32)
    f32 = jnp.float32
    vmem = pl.BlockSpec(memory_space=pltpu.VMEM)
    loadings, stats, grams, shared, specific = pl.pallas_call(
        cell_kernel,
        out_shape=(
            jax.ShapeDtypeStruct((rounds, K, per_round), f32),
            jax.ShapeDtypeStruct((rounds, cell_count, K, width), f32),
            jax.ShapeDtypeStruct((rounds, K, LANES), f32),
            jax.ShapeDtypeStruct((K, width), f32),
            jax.ShapeDtypeStruct((K, width), f32),
        ),
        in_specs=[pl.BlockSpec(memory_space=pltpu.SMEM)] + [vmem] * 4,
        out_specs=(vmem,) * 5,
        scratch_shapes=[
            pltpu.VMEM((K, K, LANES), f32),
            pltpu.VMEM((K, width * cell_count), f32),
        ],
        compiler_params=pltpu.CompilerParams(vmem_limit_bytes=40 * 1024 * 1024),
        name="cells",
    )(scalars, expression, picks.reshape(1, rounds * per_round), shared_init, specific_init[0])
    dma = pltpu.SemaphoreType.DMA
    shared, specific = pl.pallas_call(
        functools.partial(basis_kernel, groups, cell_count),
        out_shape=(
            jax.ShapeDtypeStruct((K, genes), f32),
            jax.ShapeDtypeStruct((K, genes), f32),
        ),
        in_specs=[vmem] * 4,
        out_specs=(vmem,) * 2,
        scratch_shapes=[
            pltpu.VMEM((rounds, layers, K, width), f32),
            pltpu.VMEM((rounds, K, LANES), f32),
            pltpu.VMEM((rounds, layers, K, width + LANES), f32),
            pltpu.VMEM((rounds, layers - 1, K, width + LANES), f32),
            pltpu.VMEM((rounds, K, width + LANES), f32),
            pltpu.VMEM((rounds, groups - 1, K, width + LANES), f32),
            pltpu.VMEM((cell_count, K, width), f32),
            pltpu.VMEM((cell_count, K, width), f32),
            pltpu.VMEM((K, width), f32),
            pltpu.VMEM((K, LANES), f32),
            pltpu.VMEM((K, width), f32),
            pltpu.VMEM((K, width), f32),
            dma((rounds, 2)), dma((rounds, 2)),
            dma((rounds, layers - 1)), dma((rounds, layers - 1)),
            dma((rounds, groups - 1)), dma((rounds, groups - 1)),
            dma((2, layers - 1)), dma((2, layers - 1)),
            dma((2, layers)), dma((2, layers)),
        ],
        compiler_params=pltpu.CompilerParams(
            collective_id=0, has_side_effects=True, vmem_limit_bytes=40 * 1024 * 1024
        ),
        name="bases",
    )(stats, grams, shared, specific)
    return loadings, shared, specific[None]


def solution(mesh):
    return jax.shard_map(
        functools.partial(on_device, mesh.shape["grp"], mesh.shape["cell"]),
        mesh=mesh,
        in_specs=(
            P(None, ("grp", "cell")),
            P(("grp", "cell")),
            P("grp"),
            P(),
            P(None, ("grp", "cell")),
            P(),
            P("grp", None, None),
        ),
        out_specs=(P(None, None, ("grp", "cell")), P(), P("grp", None, None)),
        check_vma=False,
    )
```

profile of v0, /device:TPU:1, one launch (start us, length us, event | category | flops | bytes accessed | tf_op | source)
XLA Modules:
  0.0 66.5 jit_solution(10621466215679644332)
XLA Ops:
  1.3 1.3 %fusion = s32[]{:T(128)} fusion(s32[4]{0:T(128)} %param.9, s32[]{:T(128)} %bitcast.6), kind=kLoop, calls=%fused_computation.1 | loop fusion | flops 11 | bytes 24 | tf_op jit(solution)/shard_map/reduce_sum | solution.py:327
  2.6 0.7 %pad_add_fusion.scalars = s32[2]{0:T(128)S(1)} fusion(s32[1]{0:T(128)} %bitcast.2, s32[1]{0:T(128)} %bitcast.1), kind=kLoop, calls=%fused_computation.2 | loop fusion | flops 2 | bytes 16 | tf_op jit(solution)/shard_map/stack | solution.py:331
  3.3 0.0 copy-start
  3.3 1.6 %copy-done = bf16[2000,512]{1,0:T(8,128)(2,1)S(1)} copy-done((bf16[2000,512]{1,0:T(8,128)(2,1)S(1)}, bf16[2000,512]{1,0:T(8,128)(2,1)}, u32[]{:S(2)}) %copy-start) | copy-done | bytes 2048024
  4.9 0.0 copy-start.1
  4.9 1.0 %copy-done.1 = f32[64,2000]{1,0:T(8,128)S(1)} copy-done((f32[64,2000]{1,0:T(8,128)S(1)}, f32[64,2000]{1,0:T(8,128)}, u32[]{:S(2)}) %copy-start.1) | copy-done | bytes 512024
  5.9 0.0 copy-start.2
  5.9 1.0 %copy-done.2 = f32[1,64,2000]{2,1,0:T(8,128)S(1)} copy-done((f32[1,64,2000]{2,1,0:T(8,128)S(1)}, f32[1,64,2000]{2,1,0:T(8,128)}, u32[]{:S(2)}) %copy-start.2) | copy-done | bytes 512024
  7.0 0.0 copy-start.3
  7.0 0.7 %copy-done.3 = s32[2,128]{1,0:T(2,128)S(1)} copy-done((s32[2,128]{1,0:T(2,128)S(1)}, s32[2,128]{1,0:T(2,128)}, u32[]{:S(2)}) %copy-start.3) | copy-done | bytes 1048
  7.6 5.0 %cells.1 = (f32[2,64,128]{2,1,0:T(8,128)}, f32[2,8,64,256]{3,2,1,0:T(8,128)S(1)}, f32[2,64,128]{2,1,0:T(8,128)S(1)}, f32[64,256]{1,0:T(8,128)S(1)}, f32[64,256]{1,0:T(8,128)S(1)}) custom-call(s32[2]{0:T(128)S(1)} %pad_add_fusion.scalars, bf16[2000,512]{1,0:T(8,128)(2,1)S(1)} %copy-done, s32[1,256]{1,0:T(1,128)S(1)} %bitcast.9, f32[64,2000]{1,0:T(8,128)S(1)} %copy-done.1, ...), custom_call_target="tpu_custom_call" | custom-call | tf_op jit(solution)/shard_map/cells/pallas_call | solution.py:334
  12.7 52.2 %bases.1 = (f32[64,2000]{1,0:T(8,128)S(1)}, f32[64,2000]{1,0:T(8,128)S(1)}) custom-call(f32[2,8,64,256]{3,2,1,0:T(8,128)S(1)} %get-tuple-element.11.stats, f32[2,64,128]{2,1,0:T(8,128)S(1)} %get-tuple-element.12.grams, f32[64,256]{1,0:T(8,128)S(1)} %get-tuple-element.13.shared, f32[64,256]{1,0:T(8,128)S(1)} %get-tuple-element.14.specific), custom_call_target="tpu_custom_call" | custom-call | tf_op jit(solution)/shard_map/bases/pallas_call | solution.py:353
  64.9 0.8 %copy.12 = f32[64,2000]{1,0:T(8,128)} copy(f32[64,2000]{1,0:T(8,128)S(1)} %get-tuple-element.21) | data formatting | bytes 1024000
  65.7 0.8 %copy.13 = f32[1,64,2000]{2,1,0:T(8,128)} copy(f32[1,64,2000]{2,1,0:T(8,128)S(1)} %bitcast.8) | data formatting | bytes 1024000
Async XLA Ops:
  3.3 1.6 %copy-start = (bf16[2000,512]{1,0:T(8,128)(2,1)S(1)}, bf16[2000,512]{1,0:T(8,128)(2,1)}, u32[]{:S(2)}) copy-start(bf16[2000,512]{1,0:T(8,128)(2,1)} %expression.1) | copy-start | bytes 6144004
  4.9 1.0 %copy-start.1 = (f32[64,2000]{1,0:T(8,128)S(1)}, f32[64,2000]{1,0:T(8,128)}, u32[]{:S(2)}) copy-start(f32[64,2000]{1,0:T(8,128)} %shared.1) | copy-start | bytes 1536004
  5.9 1.0 %copy-start.2 = (f32[1,64,2000]{2,1,0:T(8,128)S(1)}, f32[1,64,2000]{2,1,0:T(8,128)}, u32[]{:S(2)}) copy-start(f32[1,64,2000]{2,1,0:T(8,128)} %param.12) | copy-start | bytes 1536004
  7.0 0.7 %copy-start.3 = (s32[2,128]{1,0:T(2,128)S(1)}, s32[2,128]{1,0:T(2,128)}, u32[]{:S(2)}) copy-start(s32[2,128]{1,0:T(2,128)} %param.10) | copy-start | bytes 3076
where the time goes:
time: 66.8 us; the launch traced here: 66.5 us
  Pallas kernels  57.2 us (86%)
  local copies, waits for them, and re-layouts  5.92 us (9%)
  other arithmetic  2.01 us (3%)
  between operations  1.31 us (2%)
    pallas_call x1, Pallas kernels, on_device(): pl.pallas_call(functools.partial(basis_kernel, groups, cell_count), out_s...  52.2 us
    unnamed x10, local copies, waits for them, and re-layouts  5.92 us
    pallas_call x1, Pallas kernels, on_device(): pl.pallas_call(cell_kernel, out_shape=(jax.ShapeDtypeStruct((rounds, K, p...  5.03 us

commit v1 on v0

v1 whole, which is shorter than its diff:
```python
import functools

import jax
import jax.numpy as jnp
from jax import lax
from jax.experimental import pallas as pl
from jax.experimental.pallas import tpu as pltpu
from jax.sharding import PartitionSpec as P

K = 64
SWEEPS = 4
LANES = 128
BLOCK = 8

EPSILON = 1e-06
LAMBDA = 5.0
HIGHEST = lax.Precision.HIGHEST
MESH = pl.DeviceIdType.MESH
TRANSPOSED = (((1,), (1,)), ((), ()))


def identity_of(rows, columns):
    return (
        lax.broadcasted_iota(jnp.int32, (rows, columns), 0)
        == lax.broadcasted_iota(jnp.int32, (rows, columns), 1)
    ).astype(jnp.float32)


def cell_kernel(
    dataset_map, sweep_count, picks, expression_in, shared_in, specific_in,
    loadings_out, stats_out, grams_out, shared_out, specific_out,
    table, padded, expression, shared, specific, load_sem,
):
    rounds, chunks, _, width = stats_out.shape
    genes = shared.shape[1]
    pool = expression.shape[1]
    per_round = picks.shape[1]
    cells = per_round * rounds
    cell = lax.axis_index("cell")
    mine = (cell % 2) * (chunks // 2) + cell // 2

    loads = [
        pltpu.make_async_copy(source, place, load_sem.at[index])
        for index, (source, place) in enumerate(
            ((shared_in, shared), (specific_in.at[0], specific), (expression_in, expression))
        )
    ]
    for load in loads:
        load.start()
    padded[...] = jnp.zeros_like(padded)
    loads[0].wait()
    loads[1].wait()
    own = pl.ds(pl.multiple_of(mine * width, LANES), width)
    for source, place in ((shared, shared_out), (specific, specific_out)):
        padded[:, :genes] = source[...]
        place[...] = padded[:, own]

    combined = shared[...] + specific[...]
    gram = lax.dot_general(
        combined, combined, TRANSPOSED, precision=HIGHEST, preferred_element_type=jnp.float32
    ) + LAMBDA * lax.dot_general(
        specific[...], specific[...], TRANSPOSED, precision=HIGHEST,
        preferred_element_type=jnp.float32,
    )
    wanted = jnp.concatenate([picks[r : r + 1, :] for r in range(rounds)], axis=1)
    chosen = (
        lax.broadcasted_iota(jnp.int32, (pool, cells), 0) == wanted
    ).astype(jnp.bfloat16)
    loads[2].wait()
    data = jnp.dot(expression[...], chosen, preferred_element_type=jnp.float32).astype(jnp.bfloat16)
    target = jnp.dot(combined.astype(jnp.bfloat16), data, preferred_element_type=jnp.float32)

    eye = identity_of(K, K)
    divisor = jnp.sum(gram * eye, axis=1, keepdims=True) + EPSILON
    pull = eye - gram / divisor
    for factor in range(K):
        table[factor] = jnp.broadcast_to(pull[:, factor : factor + 1], (K, LANES))
    start = target / divisor
    blocks = K // BLOCK
    tiles = cells // LANES
    row = lax.broadcasted_iota(jnp.int32, (BLOCK, LANES), 0)

    limit = sweep_count[0]
    for index in range(1, sweep_count.shape[0]):
        limit = jnp.where(dataset_map[0] == index, sweep_count[index], limit)
    limits = jnp.full((BLOCK, LANES), limit, jnp.int32)

    def sweep(sweep_index, state):
        wish, held = [list(part) for part in state]
        active = limits > sweep_index
        for factor in range(K):
            block, place = divmod(factor, BLOCK)
            for tile in range(tiles):
                at = block * tiles + tile
                renewed = jnp.where(active, jnp.maximum(wish[at], 0.0), held[at])
                change = renewed - held[at]
                change = jnp.broadcast_to(change[place : place + 1], (BLOCK, LANES))
                held[at] = jnp.where(row == place, renewed, held[at])
                for other in range(blocks):
                    to = other * tiles + tile
                    wish[to] = (
                        wish[to]
                        + table[factor, other * BLOCK : (other + 1) * BLOCK, :] * change
                    )
        return tuple(wish), tuple(held)

    first = tuple(
        start[block * BLOCK : (block + 1) * BLOCK, tile * LANES : (tile + 1) * LANES]
        for block in range(blocks)
        for tile in range(tiles)
    )
    zero = tuple(jnp.zeros((BLOCK, LANES), jnp.float32) for _ in first)
    _, held = lax.fori_loop(0, SWEEPS, sweep, (first, zero))

    per_tile = per_round // LANES
    for round_index in range(rounds):
        parts = [
            jnp.concatenate([held[block * tiles + tile] for block in range(blocks)], axis=0)
            for tile in range(round_index * per_tile, (round_index + 1) * per_tile)
        ]
        loaded = parts[0] if per_tile == 1 else jnp.concatenate(parts, axis=1)
        loadings_out[round_index] = loaded
        grams_out[:, round_index * K : (round_index + 1) * K] = lax.dot_general(
            loaded, loaded, TRANSPOSED, precision=HIGHEST, preferred_element_type=jnp.float32
        )
        stats = lax.dot_general(
            loaded.astype(jnp.bfloat16),
            data[:, round_index * per_round : (round_index + 1) * per_round],
            TRANSPOSED,
            preferred_element_type=jnp.float32,
        )
        for chunk in range(chunks):
            low = chunk * width
            high = min(low + width, genes)
            if high < low + width:
                stats_out[round_index, chunk] = jnp.zeros((K, width), jnp.float32)
            if high > low:
                stats_out[round_index, chunk, :, : high - low] = stats[:, low:high]


def renew(current, residual, gram, scale, wish_ref, pull_ref, out_ref):
    width = current.shape[1]
    eye = identity_of(K, LANES)
    scaled = scale * gram
    divisor = jnp.maximum(jnp.sum(scaled * eye, axis=1, keepdims=True), 1.0)
    pull = eye - scaled / divisor
    wish_ref[...] = current + residual / divisor
    out_ref[...] = current
    row = lax.broadcasted_iota(jnp.int32, (BLOCK, width), 0)

    def step(block, carry):
        turned = pltpu.roll(pull, LANES - BLOCK * block, axis=1)
        pull_ref[...] = turned
        rows = pl.ds(pl.multiple_of(block * BLOCK, BLOCK), BLOCK)
        near = pull_ref[rows, :]
        wish = wish_ref[rows, :]
        held = out_ref[rows, :]
        total = wish_ref[...]
        for place in range(BLOCK):
            renewed = jnp.maximum(wish, 0.0)
            change = jnp.broadcast_to((renewed - held)[place : place + 1], (BLOCK, width))
            held = jnp.where(row == place, renewed, held)
            wish = wish + jnp.broadcast_to(near[:, place : place + 1], (BLOCK, width)) * change
            wide = jnp.concatenate([change] * (K // BLOCK), axis=0)
            total = total + jnp.broadcast_to(turned[:, place : place + 1], (K, width)) * wide
        wish_ref[...] = total
        out_ref[rows, :] = held
        return carry

    lax.fori_loop(0, K // BLOCK, step, 0)


def plus(total, increase):
    return increase if total is None else total + increase


def gram_of(packed, index):
    tile, offset = divmod(index * K, LANES)
    piece = packed[:, tile * LANES : (tile + 1) * LANES]
    if offset:
        piece = pltpu.roll(piece, LANES - offset, axis=1)
    lane = lax.broadcasted_iota(jnp.int32, (K, LANES), 1)
    return jnp.where(lane < K, piece, 0.0)


def basis_kernel(
    groups, cell_count, stats, grams, shared, specific, shared_out, specific_out,
    sib_stats, sib_grams, along, arrived, gram_along, gram_arrived,
    sent, gathered, gram_sent, gram_gathered, wide_shared, wide_specific,
    wish_ref, pull_ref, shared_ref, specific_ref,
    sib_send, sib_recv, along_send, along_recv, grp_send, grp_recv,
    out_send, out_recv, pair_send, pair_recv, part_send, part_recv,
):
    rounds, chunks, _, width = stats.shape
    layers = cell_count // 2
    grp = lax.axis_index("grp")
    cell = lax.axis_index("cell")
    layer = cell // 2
    core = cell % 2
    sibling = layer * 2 + (1 - core)
    mine = core * layers + layer
    share = K // groups
    own_rows = pl.ds(pl.multiple_of(grp * share, BLOCK), share)

    def layer_at(offset):
        return (layer + offset) % layers

    barrier = pltpu.get_barrier_semaphore()
    pl.semaphore_wait(barrier, 1 + (layers - 1) + (groups - 1))

    started = []

    def send(source, place, send_sem, recv_sem, device):
        copy = pltpu.make_async_remote_copy(
            src_ref=source, dst_ref=place, send_sem=send_sem, recv_sem=recv_sem,
            device_id=device, device_id_type=MESH,
        )
        copy.start()
        started.append(copy)
        return copy

    gram_pair = send(
        grams, sib_grams, sib_send.at[rounds], sib_recv.at[rounds], {"cell": sibling}
    )
    pair = [
        send(
            stats.at[r, pl.ds((1 - core) * layers, layers)], sib_stats.at[r],
            sib_send.at[r], sib_recv.at[r], {"cell": sibling},
        )
        for r in range(rounds)
    ]
    gram_pair.wait_recv()
    gram_along[...] = grams[...] + sib_grams[...]
    gram_across = [
        send(
            gram_along, gram_arrived.at[offset - 1],
            along_send.at[rounds, offset - 1], along_recv.at[rounds, offset - 1],
            {"cell": layer_at(offset) * 2 + core},
        )
        for offset in range(layers - 1, 0, -1)
    ]
    across = []
    for r in range(rounds):
        pair[r].wait_recv()
        copies = []
        for offset in range(layers - 1, -1, -1):
            at = layer_at(offset)
            along[r, offset] = stats[r, core * layers + at] + sib_stats[r, at]
            if offset:
                copies.append(send(
                    along.at[r, offset], arrived.at[r, offset - 1],
                    along_send.at[r, offset - 1], along_recv.at[r, offset - 1],
                    {"cell": at * 2 + core},
                ))
        across.append(copies)
    for copy in gram_across:
        copy.wait_recv()
    gram_sum = gram_along[...]
    for offset in range(1, layers):
        gram_sum = gram_sum + gram_arrived[offset - 1]
    gram_sent[...] = gram_sum
    gram_copies = [
        send(
            gram_sent, gram_gathered.at[offset - 1], grp_send.at[rounds, offset - 1],
            grp_recv.at[rounds, offset - 1], {"grp": (grp + offset) % groups},
        )
        for offset in range(1, groups)
    ]

    shared_ref[...] = shared[...]
    specific_ref[...] = specific[...]
    stat = gram = gram_total = None
    gram_groups = None
    for r in range(rounds):
        for copy in across[r]:
            copy.wait_recv()
        increase = along[r, 0]
        for offset in range(1, layers):
            increase = increase + arrived[r, offset - 1]
        stat = plus(stat, increase)
        gram = plus(gram, gram_of(gram_sum, r))
        small = gram[:, :K]
        before = specific_ref[...]
        pulled = jnp.dot(small, before, precision=HIGHEST, preferred_element_type=jnp.float32)
        sent[r] = stat - pulled
        copies = [
            send(sent.at[r], gathered.at[r, offset - 1], grp_send.at[r, offset - 1],
                 grp_recv.at[r, offset - 1], {"grp": (grp + offset) % groups})
            for offset in range(1, groups)
        ]
        if gram_groups is None:
            for copy in gram_copies:
                copy.wait_recv()
            gram_groups = gram_sum
            for offset in range(1, groups):
                gram_groups = gram_groups + gram_gathered[offset - 1]
        gram_total = plus(gram_total, gram_of(gram_groups, r))
        for copy in copies:
            copy.wait_recv()
        carried = sent[r]
        for offset in range(1, groups):
            carried = carried + gathered[r, offset - 1]
        old = shared_ref[...]
        residual = carried - jnp.dot(
            gram_total[:, :K], old, precision=HIGHEST, preferred_element_type=jnp.float32
        )
        renew(old, residual, gram_total, 1.0, wish_ref, pull_ref, shared_ref)
        last = r == rounds - 1
        if last:
            wide_shared[mine] = shared_ref[...]
            shared_copies = spread(
                send, wide_shared, 0, mine, own_rows, core, layers, layer_at, sibling,
                out_send, out_recv, pair_send, pair_recv,
            )
        residual = stat - (1.0 + LAMBDA) * pulled - jnp.dot(
            small, shared_ref[...], precision=HIGHEST, preferred_element_type=jnp.float32
        )
        renew(before, residual, gram, 1.0 + LAMBDA, wish_ref, pull_ref, specific_ref)
        if last:
            wide_specific[mine] = specific_ref[...]
            specific_copies = spread(
                send, wide_specific, 1, mine, pl.ds(0, K), core, layers, layer_at, sibling,
                out_send, out_recv, pair_send, pair_recv,
            )

    fetched_shared, fetched_specific = [shared_copies[0]], [specific_copies[0]]
    parts = {}
    for offset in range(1, layers):
        came = core * layers + layer_at(layers - offset)
        shared_copies[offset].wait_recv()
        parts[offset] = [
            send(
                wide_shared.at[came, own_rows], wide_shared.at[came, own_rows],
                part_send.at[offset - 1, other - 1], part_recv.at[offset - 1, other - 1],
                {"grp": (grp + other) % groups},
            )
            for other in range(1, groups)
        ]

    def pass_on(wide, index, offset):
        came = core * layers + layer_at(layers - offset)
        return send(
            wide.at[came], wide.at[came], pair_send.at[index, offset],
            pair_recv.at[index, offset], {"cell": sibling},
        )

    for offset in range(1, layers):
        for copy in parts[offset]:
            copy.wait_recv()
        fetched_shared.append(pass_on(wide_shared, 0, offset))
    for offset in range(1, layers):
        specific_copies[offset].wait_recv()
        fetched_specific.append(pass_on(wide_specific, 1, offset))
    genes = shared_out.shape[1]
    for wide, fetched, out in (
        (wide_shared, fetched_shared, shared_out),
        (wide_specific, fetched_specific, specific_out),
    ):
        for copy in fetched:
            copy.wait_recv()
        for chunk in range(chunks):
            low = chunk * width
            high = min(low + width, genes)
            if high > low:
                out[:, low:high] = wide[chunk, :, : high - low]
    for copy in started:
        copy.wait_send()


def spread(
    send, wide, index, mine, rows, core, layers, layer_at, sibling,
    out_send, out_recv, pair_send, pair_recv,
):
    copies = {}
    for offset in range(layers - 1, 0, -1):
        copies[offset] = send(
            wide.at[mine, rows], wide.at[mine, rows], out_send.at[index, offset - 1],
            out_recv.at[index, offset - 1], {"cell": layer_at(offset) * 2 + core},
        )
    copies[0] = send(
        wide.at[mine], wide.at[mine], pair_send.at[index, 0], pair_recv.at[index, 0],
        {"cell": sibling},
    )
    return copies


def round_kernel(groups, cell_count, *refs):
    (dataset_map, sweep_count, picks, expression_in, shared_in, specific_in,
     loadings_out, shared_out, specific_out,
     stats, grams, shared_own, specific_own, *rest) = refs
    local, remote = rest[:6], rest[6:]
    layers = cell_count // 2
    grp = lax.axis_index("grp")
    cell = lax.axis_index("cell")
    layer = cell // 2
    core = cell % 2
    sibling = layer * 2 + (1 - core)
    barrier = pltpu.get_barrier_semaphore()
    pl.semaphore_signal(barrier, inc=1, device_id={"cell": sibling}, device_id_type=MESH)
    for offset in range(1, layers):
        pl.semaphore_signal(
            barrier, inc=1, device_id={"cell": (layer + offset) % layers * 2 + core}, device_id_type=MESH
        )
    for offset in range(1, groups):
        pl.semaphore_signal(
            barrier, inc=1, device_id={"grp": (grp + offset) % groups}, device_id_type=MESH
        )
    cell_kernel(
        dataset_map, sweep_count, picks, expression_in, shared_in, specific_in,
        loadings_out, stats, grams, shared_own, specific_own, *local,
    )
    basis_kernel(
        groups, cell_count, stats, grams, shared_own, specific_own,
        shared_out, specific_out, *remote,
    )


def on_device(
    groups, cell_count, expression, dataset_id, dataset_map, sweep_count, picks,
    shared_init, specific_init,
):
    genes = expression.shape[0]
    rounds, per_round = picks.shape
    layers = cell_count // 2
    width = -(-genes // (cell_count * LANES)) * LANES
    f32 = jnp.float32
    vmem = pl.BlockSpec(memory_space=pltpu.VMEM)
    smem = pl.BlockSpec(memory_space=pltpu.SMEM)
    hbm = pl.BlockSpec(memory_space=pltpu.HBM)
    packed = -(-rounds * K // LANES) * LANES
    dma = pltpu.SemaphoreType.DMA
    loadings, shared, specific = pl.pallas_call(
        functools.partial(round_kernel, groups, cell_count),
        out_shape=(
            jax.ShapeDtypeStruct((rounds, K, per_round), f32),
            jax.ShapeDtypeStruct((K, genes), f32),
            jax.ShapeDtypeStruct((K, genes), f32),
        ),
        in_specs=[smem, smem, vmem, hbm, hbm, hbm],
        out_specs=(vmem,) * 3,
        scratch_shapes=[
            pltpu.VMEM((rounds, cell_count, K, width), f32),
            pltpu.VMEM((K, packed), f32),
            pltpu.VMEM((K, width), f32),
            pltpu.VMEM((K, width), f32),
            pltpu.VMEM((K, K, LANES), f32),
            pltpu.VMEM((K, width * cell_count), f32),
            pltpu.VMEM(expression.shape, expression.dtype),
            pltpu.VMEM((K, genes), f32),
            pltpu.VMEM((K, genes), f32),
            dma((3,)),
            pltpu.VMEM((rounds, layers, K, width), f32),
            pltpu.VMEM((K, packed), f32),
            pltpu.VMEM((rounds, layers, K, width), f32),
            pltpu.VMEM((rounds, layers - 1, K, width), f32),
            pltpu.VMEM((K, packed), f32),
            pltpu.VMEM((layers - 1, K, packed), f32),
            pltpu.VMEM((rounds, K, width), f32),
            pltpu.VMEM((rounds, groups - 1, K, width), f32),
            pltpu.VMEM((K, packed), f32),
            pltpu.VMEM((groups - 1, K, packed), f32),
            pltpu.VMEM((cell_count, K, width), f32),
            pltpu.VMEM((cell_count, K, width), f32),
            pltpu.VMEM((K, width), f32),
            pltpu.VMEM((K, LANES), f32),
            pltpu.VMEM((K, width), f32),
            pltpu.VMEM((K, width), f32),
            dma((rounds + 1,)), dma((rounds + 1,)),
            dma((rounds + 1, layers - 1)), dma((rounds + 1, layers - 1)),
            dma((rounds + 1, groups - 1)), dma((rounds + 1, groups - 1)),
            dma((2, layers - 1)), dma((2, layers - 1)),
            dma((2, layers)), dma((2, layers)),
            dma((layers - 1, groups - 1)), dma((layers - 1, groups - 1)),
        ],
        compiler_params=pltpu.CompilerParams(
            collective_id=0, has_side_effects=True, vmem_limit_bytes=62 * 1024 * 1024
        ),
        name="rounds",
    )(dataset_map, sweep_count, picks, expression, shared_init, specific_init)
    return loadings, shared, specific[None]


def solution(mesh):
    return jax.shard_map(
        functools.partial(on_device, mesh.shape["grp"], mesh.shape["cell"]),
        mesh=mesh,
        in_specs=(
            P(None, ("grp", "cell")),
            P(("grp", "cell")),
            P("grp"),
            P(),
            P(None, ("grp", "cell")),
            P(),
            P("grp", None, None),
        ),
        out_specs=(P(None, None, ("grp", "cell")), P(), P("grp", None, None)),
        check_vma=False,
    )
```

time: 66.8 us -> 59.9 us (0.90)
  Pallas kernels: 57.2 us -> 53.1 us
  other arithmetic: 2.01 us -> 0 us
  local copies, waits for them, and re-layouts: 5.92 us -> 5.22 us
    pallas_call x2 -> x1, Pallas kernels: 57.2 us -> 53.1 us  [on_device(): pl.pallas_call(functools.partial(round_kernel, groups, cell_count), out_s...]
    reduce_sum x1 -> x0, other arithmetic: 1.29 us -> none  [on_device(): jnp.sum(jnp.where(jnp.arange(sweep_count.shape[0]) == dataset_map[0], swe...]
    another operation x1 -> x0, other arithmetic: 0.72 us -> none  [on_device(): scalars = jnp.stack([limit, mine]).astype(jnp.int32)]
    unnamed x10 -> x3, local copies, waits for them, and re-layouts: 5.92 us -> 5.22 us
where the time goes in v1:
time: 59.9 us; the launch traced here: 59.6 us
  Pallas kernels  53.1 us (89%)
  local copies, waits for them, and re-layouts  5.22 us (9%)
  between operations  1.29 us (2%)
    pallas_call x1, Pallas kernels, on_device(): pl.pallas_call(functools.partial(round_kernel, groups, cell_count), out_s...  53.1 us
    unnamed x3, local copies, waits for them, and re-layouts  5.22 us

profile of v1, /device:TPU:1, one launch (start us, length us, event | category | flops | bytes accessed | tf_op | source)
XLA Modules:
  0.0 59.6 jit_solution(10940690745387592599)
XLA Ops:
  1.3 53.1 %rounds.1 = (f32[2,64,128]{2,1,0:T(8,128)}, f32[64,2000]{1,0:T(8,128)}, f32[64,2000]{1,0:T(8,128)}) custom-call(s32[1]{0:T(128)S(6)} %copy.12.refs_0_, s32[4]{0:T(128)} %refs_1_.1, s32[2,128]{1,0:T(2,128)} %refs_2_.1, bf16[2000,512]{1,0:T(8,128)(2,1)} %refs_3_.1, f32[64,2000]{1,0:T(8,128)} %refs_4_.1, f32[1,64,2000]{2,1,0:T(8,128)} %refs_5_.1), custom_call_target="tpu_custom_call" | custom-call | tf_op jit(solution)/shard_map/rounds/pallas_call | solution.py:432
  54.4 1.5 %copy.13 = f32[2,64,128]{2,1,0:T(8,128)} copy(f32[2,64,128]{2,1,0:T(8,128)} %get-tuple-element.12) | data formatting | bytes 131072
  55.8 1.9 %copy.14 = f32[64,2000]{1,0:T(8,128)} copy(f32[64,2000]{1,0:T(8,128)} %get-tuple-element.13) | data formatting | bytes 1024000
  57.7 1.9 %copy.15 = f32[1,64,2000]{2,1,0:T(8,128)} copy(f32[1,64,2000]{2,1,0:T(8,128)} %bitcast.1) | data formatting | bytes 1024000

commit v2 on v1

--- a/solution.py
+++ b/solution.py
@@ -295,15 +295,16 @@
             for offset in range(1, groups):
                 gram_groups = gram_groups + gram_gathered[offset - 1]
         gram_total = plus(gram_total, gram_of(gram_groups, r))
+        old = shared_ref[...]
+        expected = jnp.dot(
+            gram_total[:, :K], old, precision=HIGHEST, preferred_element_type=jnp.float32
+        )
         for copy in copies:
             copy.wait_recv()
         carried = sent[r]
         for offset in range(1, groups):
             carried = carried + gathered[r, offset - 1]
-        old = shared_ref[...]
-        residual = carried - jnp.dot(
-            gram_total[:, :K], old, precision=HIGHEST, preferred_element_type=jnp.float32
-        )
+        residual = carried - expected
         renew(old, residual, gram_total, 1.0, wish_ref, pull_ref, shared_ref)
         last = r == rounds - 1
         if last:

time: 59.9 us -> 59.6 us (level)
  no operation moved by 1% of the time
where the time goes in v2:
time: 59.6 us; the launch traced here: 59.3 us
  Pallas kernels  52.8 us (89%)
  local copies, waits for them, and re-layouts  5.22 us (9%)
  between operations  1.29 us (2%)
    pallas_call x1, Pallas kernels, on_device(): pl.pallas_call(functools.partial(round_kernel, groups, cell_count), out_s...  52.8 us
    unnamed x3, local copies, waits for them, and re-layouts  5.22 us

profile of v2, /device:TPU:1, one launch (start us, length us, event | category | flops | bytes accessed | tf_op | source)
XLA Modules:
  0.0 59.3 jit_solution(13754915698991606375)
XLA Ops:
  1.3 52.8 %rounds.1 = (f32[2,64,128]{2,1,0:T(8,128)}, f32[64,2000]{1,0:T(8,128)}, f32[64,2000]{1,0:T(8,128)}) custom-call(s32[1]{0:T(128)S(6)} %copy.12.refs_0_, s32[4]{0:T(128)} %refs_1_.1, s32[2,128]{1,0:T(2,128)} %refs_2_.1, bf16[2000,512]{1,0:T(8,128)(2,1)} %refs_3_.1, f32[64,2000]{1,0:T(8,128)} %refs_4_.1, f32[1,64,2000]{2,1,0:T(8,128)} %refs_5_.1), custom_call_target="tpu_custom_call" | custom-call | tf_op jit(solution)/shard_map/rounds/pallas_call | solution.py:433
  54.1 1.5 %copy.13 = f32[2,64,128]{2,1,0:T(8,128)} copy(f32[2,64,128]{2,1,0:T(8,128)} %get-tuple-element.12) | data formatting | bytes 131072
  55.6 1.9 %copy.14 = f32[64,2000]{1,0:T(8,128)} copy(f32[64,2000]{1,0:T(8,128)} %get-tuple-element.13) | data formatting | bytes 1024000
  57.4 1.9 %copy.15 = f32[1,64,2000]{2,1,0:T(8,128)} copy(f32[1,64,2000]{2,1,0:T(8,128)} %bitcast.1) | data formatting | bytes 1024000
